TPU v7x, 512 devices: a whole 4x4x16 slice. The times are simulated.
512 devices in a mesh: vox: 64 (over z, x_hi, core), tm: 4 (over y), mod: 2 (over x_lo).
Axes of the slice: x: 4 (x_hi: 2, x_lo: 2; x = x_hi * 2 + x_lo), y: 4, z: 16, core: 2. Of those that a mesh axis runs over, the one named last changes fastest.
Arguments:
- scans: bfloat16 [2, 16384, 48, 512], P('mod', 'vox', None, 'tm'), may hold values from -6 to 6
- spatial_init: float32 [2, 16384, 128], P('mod', 'vox'), may hold values from -6 to 6
- time_init: float32 [512, 128], P('tm'), may hold values from -0.09375 to 0.09375
- subject_init: float32 [48, 128], replicated, may hold values from -6 to 6
- hrf_kernel: float32 [16], replicated, may hold values from 0.05 to 0.5
- kept_blocks: int32 [48, 32], P(None, 'tm'), may hold values 0 or 1
Outputs:
- spatial_factors: float32 [2, 16384, 128], P('mod', 'vox')
- time_factors: float32 [512, 128], P('tm')
- subject_factors: float32 [48, 128], replicated
All inputs are finite; a program needn't handle non-finite values. No bound on the sum of `kept_blocks` on one device may be relied on, other than what follows from the above.
Results may differ from a plain program's by a relative error of at most 0.003.
Values sent between devices are 32-bit elements; how exact they have to be, the bound alone decides.
A program may use at most 64 MiB of HBM per device.

v0:
```python
import jax
import jax.numpy as jnp
from jax import lax
from jax.sharding import PartitionSpec as P

RIDGE = 0.1
EPS = 1e-06


def shifted(block, axis, distance):
    devices = range(lax.axis_size(axis))
    route = [(i - distance, i) for i in devices if i - distance in devices]
    return lax.ppermute(block, axis, route)


def ridge_solve(right_side, gram):
    eye_mat = jnp.eye(gram.shape[0], dtype=gram.dtype)
    factor = jnp.linalg.cholesky(gram + RIDGE * eye_mat)
    return jax.scipy.linalg.cho_solve((factor, True), right_side.T).T


def hgram(left, right):
    return jnp.dot(left.T, right, precision=lax.Precision.HIGHEST)


def conv_causal(series, kernel):
    reach = kernel.shape[0]
    count = series.shape[0]
    tail_part = series[count - (reach - 1) :]
    before = shifted(tail_part, "tm", 1)
    padded = jnp.concatenate([before, series])
    summed = jnp.zeros_like(series)
    for lag in range(reach):
        summed = summed + kernel[lag] * padded[reach - 1 - lag : reach - 1 - lag + count]
    return summed


def conv_adjoint(series, kernel):
    reach = kernel.shape[0]
    count = series.shape[0]
    head_part = series[: reach - 1]
    after = shifted(head_part, "tm", -1)
    padded = jnp.concatenate([series, after])
    summed = jnp.zeros_like(series)
    for lag in range(reach):
        summed = summed + kernel[lag] * padded[lag : lag + count]
    return summed


def per_device(scans, spatial_init, time_init, subject_init, hrf_kernel, kept_blocks):
    is_fmri = lax.axis_index("mod") == 0
    row_count, subj_count, tr_count = (scans.shape[1], scans.shape[2], scans.shape[3])
    rank_count = subject_init.shape[1]
    total_rows = row_count * lax.axis_size("vox")
    total_trs = tr_count * lax.axis_size("tm")
    factor_t = jnp.where(is_fmri, conv_causal(time_init, hrf_kernel), time_init)
    block_len = tr_count // kept_blocks.shape[1]
    kept_tr = jnp.logical_or(
        jnp.repeat(kept_blocks, block_len, axis=1) > 0, jnp.logical_not(is_fmri)
    )
    khatri = (
        (subject_init[:, None, :] * factor_t[None, :, :])
        .astype(jnp.bfloat16)
        .reshape(subj_count * tr_count, rank_count)
    )
    signal = scans[0].reshape(row_count, subj_count * tr_count)
    previous = spatial_init[0].astype(jnp.bfloat16)
    modeled = lax.dot_general(
        previous, khatri, (((1,), (1,)), ((), ())), preferred_element_type=jnp.float32
    )
    filled = jnp.where(
        kept_tr.reshape(1, subj_count * tr_count), signal.astype(jnp.float32), modeled
    ).astype(jnp.bfloat16)
    mttkrp_part = jnp.dot(filled, khatri, preferred_element_type=jnp.float32)
    tgram_part = hgram(factor_t, factor_t)
    mttkrp, time_gram = lax.psum((mttkrp_part, tgram_part), "tm")
    subj_gram = hgram(subject_init, subject_init)
    updated = ridge_solve(mttkrp, subj_gram * time_gram)
    rgram_part = hgram(updated, updated)
    khatri2 = (
        (updated[:, None, :] * subject_init[None, :, :])
        .astype(jnp.bfloat16)
        .reshape(row_count * subj_count, rank_count)
    )
    proj = lax.dot_general(
        filled.reshape(row_count * subj_count, tr_count),
        khatri2,
        (((0,), (0,)), ((), ())),
        preferred_element_type=jnp.float32,
    )
    adjoint = jnp.where(is_fmri, conv_adjoint(proj, hrf_kernel), proj)
    tgram_terms = rgram_part * subj_gram
    time_rhs, gram_t = lax.psum((adjoint, tgram_terms), ("vox", "mod"))
    raw = total_rows * ridge_solve(time_rhs, gram_t)
    sumsq = lax.psum(jnp.sum(raw * raw, axis=0), "tm")
    time_factors = raw / jnp.sqrt(sumsq / total_trs + EPS)
    scale_c = (2.0 * total_rows * total_trs) ** (-0.5)
    scaled_eeg = time_factors * scale_c
    scaled_t = jnp.where(is_fmri, conv_causal(scaled_eeg, hrf_kernel), scaled_eeg)
    khatri3 = (updated[:, None, :] * scaled_t[None, :, :]).astype(jnp.bfloat16)
    subj_part = lax.dot_general(
        filled.reshape(row_count, subj_count, tr_count),
        khatri3,
        (((0, 2), (0, 1)), ((), ())),
        preferred_element_type=jnp.float32,
    )
    sgram_part = hgram(scaled_t, scaled_t)
    row_gram = lax.psum(rgram_part, "vox")
    scaled_gram = lax.psum(sgram_part, "tm")
    leading = jnp.logical_and(lax.axis_index("vox") == 0, lax.axis_index("tm") == 0)
    gram_term = jnp.where(leading, row_gram * scaled_gram, 0.0)
    subject_rhs, gram_c = lax.psum((subj_part, gram_term), ("vox", "tm", "mod"))
    subject_factors = ridge_solve(subject_rhs, gram_c)
    return (updated[None], time_factors, subject_factors)


def solution(mesh):
    return jax.shard_map(
        per_device,
        mesh=mesh,
        in_specs=(
            P("mod", "vox", None, "tm"),
            P("mod", "vox", None),
            P("tm", None),
            P(),
            P(),
            P(None, "tm"),
        ),
        out_specs=(P("mod", "vox", None), P("tm", None), P()),
        check_vma=False,
    )
```

profile of v0, /device:TPU:1, one launch (start us, length us, event | category | flops | bytes accessed | tf_op | source)
XLA Modules:
  0.0 1485.5 jit_solution(1407539403140570844)
XLA Ops:
  7.2 0.7 slice.266
  7.9 4.0 collective-permute-start
  11.9 0.7 compare_or_fusion
  12.6 1.9 fusion.160
  14.6 5.1 copy.23
  20.1 10.2 fusion.98
  30.3 0.9 fusion.162
  31.6 4.8 fusion.4
  36.4 1.7 fusion.163
  38.4 3.1 copy.26
  41.5 5.7 reshape.87
  47.2 50.4 %all-reduce.16.cloned.1.call-done = (f32[256,128]{1,0:T(8,128)}, f32[128,128]{1,0:T(8,128)}) async-done(((f32[256,128]{1,0:T(8,128)}, f32[128,128]{1,0:T(8,128)}), (f32[256,128]{1,0:T(8,128)}, f32[128,128]{1,0:T(8,128)})) %all-reduce.16.cloned.1.call-update) | async-done | bytes 196624 | tf_op jit(solution)/shard_map/psum | solution.py:76
  97.6 1.1 select_add_fusion.2
  99.0 11.7 cholesky.59
  111.4 0.7 fusion.138
  112.0 9.8 custom-call.23
  121.9 1.2 fusion.156
  124.0 1.3 copy-done
  125.3 1.0 fusion.164
  126.4 1.3 collective-permute-start.1
  127.7 0.9 fusion.161
  128.6 2.2 collective-permute-done.1
  130.8 10.8 fusion.54
  141.9 322.2 %all-reduce.14.cloned.1.call-done = (f32[128,128]{1,0:T(8,128)}, f32[128,128]{1,0:T(8,128)}) async-done(((f32[128,128]{1,0:T(8,128)}, f32[128,128]{1,0:T(8,128)}), (f32[128,128]{1,0:T(8,128)}, f32[128,128]{1,0:T(8,128)})) %all-reduce.14.cloned.1.call-update) | async-done | bytes 131088 | tf_op jit(solution)/shard_map/psum | solution.py:93
  464.0 0.9 select_add_fusion.1
  465.0 0.9 fusion.152
  465.8 0.7 copy.25
  466.6 12.5 cholesky.70
  479.8 1.3 fusion.139
  481.1 10.6 custom-call.24
  491.7 1.1 fusion.150
  493.2 8.5 psum.67
  502.3 1.3 collective-permute-start.2
  504.4 10.4 fusion.10
  514.7 0.9 fusion.165
  515.7 3.5 copy.32
  519.2 0.8 copy.31
  519.9 429.4 %all-reduce.8.cloned.1.call-done = f32[128,128]{1,0:T(8,128)} async-done(((f32[128,128]{1,0:T(8,128)}), f32[128,128]{1,0:T(8,128)}) %all-reduce.8.cloned.1.call-update) | async-done | bytes 65552 | tf_op jit(solution)/shard_map/psum | solution.py:108
  949.3 54.3 %all-reduce.10.cloned.1.call-done = f32[128,128]{1,0:T(8,128)} async-done(((f32[128,128]{1,0:T(8,128)}), f32[128,128]{1,0:T(8,128)}) %all-reduce.10.cloned.1.call-update) | async-done | bytes 65552 | tf_op jit(solution)/shard_map/psum | solution.py:109
  1003.6 1.5 multiply_select_fusion
  1005.2 3.2 fusion.5
  1008.4 106.8 %psum.71 = f32[48,128]{1,0:T(8,128)S(1)} all-reduce(f32[48,128]{1,0:T(8,128)S(1)} %fusion.5), channel_id=1, replica_groups=mesh['vox'=64,'tm'=4,'mod'=2] {'vox','tm','mod'}, use_global_device_ids=true, to_apply=%region_11.13 | all-reduce | flops 6144 | bytes 49152 | tf_op jit(solution)/shard_map/psum | solution.py:112
  1115.1 337.9 %all-reduce.12.cloned.1.call-done = f32[128,128]{1,0:T(8,128)} async-done(((f32[128,128]{1,0:T(8,128)}), f32[128,128]{1,0:T(8,128)}) %all-reduce.12.cloned.1.call-update) | async-done | bytes 65552 | tf_op jit(solution)/shard_map/psum | solution.py:112
  1453.0 0.9 select_add_fusion
  1454.0 0.9 fusion.148
  1455.0 11.7 cholesky.81
  1468.0 9.8 custom-call.25
  1478.1 0.9 fusion.144
  (45 shorter events, 6.8 us)
Async XLA Ops:
  7.2 90.5 %all-reduce.16.cloned.1.call-start = ((), (), s32[]{:S(2)}) async-start(), calls=%async_computation.4 | async-start | bytes 393216 | tf_op jit(solution)/shard_map/psum | solution.py:76
  7.9 12.2 collective-permute-start
  14.6 5.5 copy-start.3
  14.6 16.6 %copy-start.1 = (f32[48,128]{1,0:T(8,128)S(1)}, f32[48,128]{1,0:T(8,128)}, u32[]{:S(2)}) copy-start(f32[48,128]{1,0:T(8,128)} %param.10) | copy-start | bytes 73732
  14.6 17.0 %copy-start.2 = (f32[1,256,128]{2,1,0:T(8,128)S(1)}, f32[1,256,128]{2,1,0:T(8,128)}, u32[]{:S(2)}) copy-start(f32[1,256,128]{2,1,0:T(8,128)} %param.8) | copy-start | bytes 393220
  38.1 425.9 %all-reduce.14.cloned.1.call-start = ((), (), s32[]{:S(2)}) async-start(), calls=%async_computation.3 | async-start | bytes 262144 | tf_op jit(solution)/shard_map/psum | solution.py:93
  123.4 1.9 copy-start
  126.4 4.4 collective-permute-start.1
  141.6 807.7 %all-reduce.8.cloned.1.call-start = ((), (), s32[]{:S(2)}) async-start(), calls=%async_computation | async-start | bytes 131072 | tf_op jit(solution)/shard_map/psum | solution.py:108
  502.3 2.1 collective-permute-start.2
  504.3 499.4 %all-reduce.10.cloned.1.call-start = ((), (), s32[]{:S(2)}) async-start(), calls=%async_computation.1 | async-start | bytes 131072 | tf_op jit(solution)/shard_map/psum | solution.py:109
  515.7 937.4 %all-reduce.12.cloned.1.call-start = ((), (), s32[]{:S(2)}) async-start(), calls=%async_computation.2 | async-start | bytes 131072 | tf_op jit(solution)/shard_map/psum | solution.py:112
Sparse Core Ops, SparseCore 0:
  38.3 59.3 all-reduce.15
  141.7 322.2 all-reduce.13
  504.4 444.8 all-reduce.7
  951.5 52.1 all-reduce.9
  1009.8 443.1 all-reduce.11
where the time goes:
time: 1490 us
  waiting for transfers between devices  1200 us (81%)
  blocking collectives  115 us (8%)
  other arithmetic  109 us (7%)
  local copies, waits for them, and re-layouts  23.8 us (2%)
  matrix products  18.6 us (1%)
    psum x1, waiting for transfers between devices, per_device(): row_gram = lax.psum(rgram_part, 'vox')  429 us
    psum x1, waiting for transfers between devices, per_device(): subject_rhs, gram_c = lax.psum((subj_part, gram_term), ('vox', 'tm', 'mod'))  338 us
    psum x1, waiting for transfers between devices, per_device(): time_rhs, gram_t = lax.psum((adjoint, tgram_terms), ('vox', 'mod'))  322 us
    psum x1, blocking collectives, per_device(): subject_rhs, gram_c = lax.psum((subj_part, gram_term), ('vox', 'tm', 'mod'))  107 us
    psum x1, waiting for transfers between devices, per_device(): scaled_gram = lax.psum(sgram_part, 'tm')  54.3 us
    psum x1, waiting for transfers between devices, per_device(): mttkrp, time_gram = lax.psum((mttkrp_part, tgram_part), 'tm')  50.4 us
    another operation x9, other arithmetic, ridge_solve(): factor = jnp.linalg.cholesky(gram + RIDGE * eye_mat)  38 us
    another operation x6, other arithmetic, ridge_solve(): return jax.scipy.linalg.cho_solve((factor, True), right_side.T).T  32.9 us
  transfers between devices with their start and end apart: 8, of which 7 were waited for; matrix products, arithmetic and copies ran while one was open for 2% of the time, Pallas kernels for 0%

commit v1 on v0

--- a/solution.py
+++ b/solution.py
@@ -1,3 +1,4 @@
+import functools
 import jax
 import jax.numpy as jnp
 from jax import lax
@@ -5,6 +6,14 @@
 
 RIDGE = 0.1
 EPS = 1e-06
+
+
+def racks_render(vals, ax_name, dev_axis):
+    shaped = jax.lax.psum(jax.lax.psum(vals, ax_name), dev_axis)
+    return shaped
+
+
+cut_the_ways = functools.partial(racks_render, ax_name="vox", dev_axis="mod")
 
 
 def shifted(block, axis, distance):
@@ -90,7 +99,7 @@
     )
     adjoint = jnp.where(is_fmri, conv_adjoint(proj, hrf_kernel), proj)
     tgram_terms = rgram_part * subj_gram
-    time_rhs, gram_t = lax.psum((adjoint, tgram_terms), ("vox", "mod"))
+    time_rhs, gram_t = cut_the_ways((adjoint, tgram_terms))
     raw = total_rows * ridge_solve(time_rhs, gram_t)
     sumsq = lax.psum(jnp.sum(raw * raw, axis=0), "tm")
     time_factors = raw / jnp.sqrt(sumsq / total_trs + EPS)

time: 1490 us -> 1260 us (0.85)
  waiting for transfers between devices: 1200 us -> 967 us
    psum x2, waiting for transfers between devices: 752 us -> 521 us  [racks_render(): shaped = jax.lax.psum(jax.lax.psum(vals, ax_name), dev_axis)]
where the time goes in v1:
time: 1260 us
  waiting for transfers between devices  967 us (77%)
  blocking collectives  115 us (9%)
  other arithmetic  109 us (9%)
  local copies, waits for them, and re-layouts  23.8 us (2%)
  matrix products  18.6 us (1%)
  between operations  14.8 us (1%)
    psum x2, waiting for transfers between devices, racks_render(): shaped = jax.lax.psum(jax.lax.psum(vals, ax_name), dev_axis)  521 us
    psum x1, waiting for transfers between devices, per_device(): subject_rhs, gram_c = lax.psum((subj_part, gram_term), ('vox', 'tm', 'mod'))  338 us
    psum x1, blocking collectives, per_device(): subject_rhs, gram_c = lax.psum((subj_part, gram_term), ('vox', 'tm', 'mod'))  107 us
    psum x1, waiting for transfers between devices, per_device(): scaled_gram = lax.psum(sgram_part, 'tm')  55 us
    psum x1, waiting for transfers between devices, per_device(): mttkrp, time_gram = lax.psum((mttkrp_part, tgram_part), 'tm')  50.4 us
    another operation x9, other arithmetic, ridge_solve(): factor = jnp.linalg.cholesky(gram + RIDGE * eye_mat)  38 us
    another operation x6, other arithmetic, ridge_solve(): return jax.scipy.linalg.cho_solve((factor, True), right_side.T).T  32.9 us
  transfers between devices with their start and end apart: 8, of which 7 were waited for; matrix products, arithmetic and copies ran while one was open for 2% of the time, Pallas kernels for 0%

profile of v1, /device:TPU:1, one launch (start us, length us, event | category | flops | bytes accessed | tf_op | source)
XLA Modules:
  0.0 1255.8 jit_solution(7703660838256751535)
XLA Ops:
  7.2 0.7 slice.266
  7.9 4.0 collective-permute-start
  11.9 0.7 compare_or_fusion
  12.6 1.9 fusion.160
  14.6 5.1 copy.23
  20.1 10.2 fusion.98
  30.3 0.9 fusion.162
  31.6 4.8 fusion.4
  36.4 1.7 fusion.163
  38.4 3.1 copy.26
  41.5 5.7 reshape.87
  47.2 50.4 %all-reduce.15.cloned.1.call-done = (f32[256,128]{1,0:T(8,128)}, f32[128,128]{1,0:T(8,128)}) async-done(((f32[256,128]{1,0:T(8,128)}, f32[128,128]{1,0:T(8,128)}), (f32[256,128]{1,0:T(8,128)}, f32[128,128]{1,0:T(8,128)})) %all-reduce.15.cloned.1.call-update) | async-done | bytes 196624 | tf_op jit(solution)/shard_map/psum | solution.py:85
  97.6 1.1 select_add_fusion.2
  99.0 11.7 cholesky.59
  111.4 0.7 fusion.138
  112.0 9.8 custom-call.23
  121.9 1.2 fusion.156
  124.0 1.3 copy-done
  125.3 1.0 fusion.164
  126.4 1.3 collective-permute-start.1
  127.7 0.9 fusion.161
  128.6 2.2 collective-permute-done.1
  130.8 10.8 fusion.54
  141.6 476.9 %all-reduce.13.cloned.1.call-done = (f32[128,128]{1,0:T(8,128)}, f32[128,128]{1,0:T(8,128)}, f32[128,128]{1,0:T(8,128)}) async-done(((f32[128,128]{1,0:T(8,128)}, f32[128,128]{1,0:T(8,128)}, f32[128,128]{1,0:T(8,128)}), (f32[128,128]{1,0:T(8,128)}, f32[128,128]{1,0:T(8,128)}, f32[128,128]{1,0:T(8,128)})) %all-reduce.13.cloned.1.call-update) | async-done | bytes 196624 | tf_op jit(solution)/shard_map/psum | solution.py:12
  618.8 44.1 %all-reduce.17.cloned.1.call-done = (f32[128,128]{1,0:T(8,128)}, f32[128,128]{1,0:T(8,128)}) async-done(((f32[128,128]{1,0:T(8,128)}, f32[128,128]{1,0:T(8,128)}), (f32[128,128]{1,0:T(8,128)}, f32[128,128]{1,0:T(8,128)})) %all-reduce.17.cloned.1.call-update) | async-done | bytes 131088 | tf_op jit(solution)/shard_map/psum | solution.py:12
  663.0 0.9 select_add_fusion.1
  663.9 0.9 fusion.152
  664.8 0.7 copy.25
  665.5 12.5 cholesky.70
  678.8 1.3 fusion.139
  680.0 10.6 custom-call.24
  690.7 1.1 fusion.150
  692.1 8.5 psum.83
  701.2 1.3 collective-permute-start.2
  703.3 10.4 fusion.10
  713.7 0.9 fusion.165
  714.7 3.5 copy.32
  718.2 0.8 copy.31
  718.9 55.0 %all-reduce.9.cloned.1.call-done = f32[128,128]{1,0:T(8,128)} async-done(((f32[128,128]{1,0:T(8,128)}), f32[128,128]{1,0:T(8,128)}) %all-reduce.9.cloned.1.call-update) | async-done | bytes 65552 | tf_op jit(solution)/shard_map/psum | solution.py:118
  773.9 1.5 multiply_select_fusion
  775.4 3.2 fusion.5
  778.6 106.8 %psum.87 = f32[48,128]{1,0:T(8,128)S(1)} all-reduce(f32[48,128]{1,0:T(8,128)S(1)} %fusion.5), channel_id=1, replica_groups=mesh['vox'=64,'tm'=4,'mod'=2] {'vox','tm','mod'}, use_global_device_ids=true, to_apply=%region_13.15 | all-reduce | flops 6144 | bytes 49152 | tf_op jit(solution)/shard_map/psum | solution.py:121
  885.4 338.0 %all-reduce.11.cloned.1.call-done = f32[128,128]{1,0:T(8,128)} async-done(((f32[128,128]{1,0:T(8,128)}), f32[128,128]{1,0:T(8,128)}) %all-reduce.11.cloned.1.call-update) | async-done | bytes 65552 | tf_op jit(solution)/shard_map/psum | solution.py:121
  1223.4 0.9 select_add_fusion
  1224.3 0.9 fusion.148
  1225.3 11.7 cholesky.81
  1238.3 9.8 custom-call.25
  1248.4 0.9 fusion.144
  (47 shorter events, 6.9 us)
Async XLA Ops:
  7.2 90.5 %all-reduce.15.cloned.1.call-start = ((), (), s32[]{:S(2)}) async-start(), calls=%async_computation.3 | async-start | bytes 393216 | tf_op jit(solution)/shard_map/psum | solution.py:85
  7.9 12.2 collective-permute-start
  14.6 5.5 copy-start.3
  14.6 16.6 %copy-start.1 = (f32[48,128]{1,0:T(8,128)S(1)}, f32[48,128]{1,0:T(8,128)}, u32[]{:S(2)}) copy-start(f32[48,128]{1,0:T(8,128)} %param.10) | copy-start | bytes 73732
  14.6 17.0 %copy-start.2 = (f32[1,256,128]{2,1,0:T(8,128)S(1)}, f32[1,256,128]{2,1,0:T(8,128)}, u32[]{:S(2)}) copy-start(f32[1,256,128]{2,1,0:T(8,128)} %param.8) | copy-start | bytes 393220
  38.1 580.4 %all-reduce.13.cloned.1.call-start = ((), (), s32[]{:S(2)}) async-start(), calls=%async_computation.2 | async-start | bytes 393216 | tf_op jit(solution)/shard_map/psum | solution.py:12
  123.4 1.9 copy-start
  126.4 4.4 collective-permute-start.1
  141.6 521.4 %all-reduce.17.cloned.1.call-start = ((), (), s32[]{:S(2)}) async-start(), calls=%async_computation.4 | async-start | bytes 262144 | tf_op jit(solution)/shard_map/psum | solution.py:12
  618.6 155.3 %all-reduce.9.cloned.1.call-start = ((), (), s32[]{:S(2)}) async-start(), calls=%async_computation | async-start | bytes 131072 | tf_op jit(solution)/shard_map/psum | solution.py:118
  701.2 2.1 collective-permute-start.2
  714.6 508.7 %all-reduce.11.cloned.1.call-start = ((), (), s32[]{:S(2)}) async-start(), calls=%async_computation.1 | async-start | bytes 131072 | tf_op jit(solution)/shard_map/psum | solution.py:121
  714.7 59.2 %copy-start.4 = (f32[128,128]{1,0:T(8,128)S(1)}, f32[128,128]{1,0:T(8,128)}, u32[]{:S(2)}) copy-start(f32[128,128]{1,0:T(8,128)} %get-tuple-element.12) | copy-start | bytes 196612
Sparse Core Ops, SparseCore 0:
  38.3 59.3 all-reduce.14
  141.7 476.7 all-reduce.12
  621.4 41.4 all-reduce.16
  714.7 59.0 all-reduce.8
  780.1 443.2 all-reduce.10
